TPU v7x, 32 devices: a whole 2x2x4 slice. The times are simulated.
32 devices in a mesh: row: 8 (over z, y), col: 4 (over x, core).
Axes of the slice: x: 2, y: 2, z: 4, core: 2. Of those that a mesh axis runs over, the one named last changes fastest.
Arguments:
- queries: float32 [16384, 256], P(('row', 'col')), may hold values from -1 to 1
- passages: float32 [16384, 256], P(('col', 'row')), may hold values from -1 to 1
- mean_cost: float32 [1], replicated, may hold values from 1 to 3
Outputs:
- row_potential: float32 [16384], P('row')
- col_potential: float32 [16384], P('col')
All inputs are finite; a program needn't handle non-finite values.
Results may differ from a plain program's by a relative error of at most 0.0003.
Values sent between devices are 32-bit elements; how exact they have to be, the bound alone decides.
A program may use at most 256 MiB of HBM per device.

v0:
```python
import math

import jax
import jax.numpy as jnp
from jax import lax
from jax.sharding import PartitionSpec as P

ITERS = 3


def inner_costs(left, right):
    left_norms = jnp.sum(left * left, axis=1)
    right_norms = jnp.sum(right * right, axis=1)
    inner = lax.dot_general(
        left,
        right,
        (((1,), (1,)), ((), ())),
        precision=lax.Precision.HIGHEST,
        preferred_element_type=jnp.float32,
    )
    return left_norms[:, None] + right_norms[None, :] - 2.0 * inner


def logsum_col(scores):
    peak = lax.pmax(jnp.max(scores, axis=1), "col")
    totals = lax.psum(jnp.sum(jnp.exp(scores - peak[:, None]), axis=1), "col")
    return peak + jnp.log(totals)


def logsum_row(scores):
    peak = lax.pmax(jnp.max(scores, axis=0), "row")
    totals = lax.psum(jnp.sum(jnp.exp(scores - peak[None, :]), axis=0), "row")
    return peak + jnp.log(totals)


def per_device(queries, passages, mean_cost):
    entropy_scale = 0.1 * mean_cost[0]
    row_count = lax.axis_size("row")
    col_count = lax.axis_size("col")
    all_queries = queries.shape[0] * row_count * col_count
    all_passages = passages.shape[0] * row_count * col_count
    query_block = lax.all_gather(queries, "col", axis=0, tiled=True)
    cost_tile = inner_costs(query_block, lax.all_gather(passages, "row", axis=0, tiled=True))
    col_potential = jnp.zeros((cost_tile.shape[1],), jnp.float32)
    row_potential = jnp.zeros((cost_tile.shape[0],), jnp.float32)
    for repeat in range(ITERS):
        scores = (col_potential[None, :] - cost_tile) / entropy_scale
        row_potential = -entropy_scale * math.log(all_queries) - entropy_scale * logsum_col(scores)
        scores = (row_potential[:, None] - cost_tile) / entropy_scale
        col_potential = -entropy_scale * math.log(all_passages) - entropy_scale * logsum_row(scores)
    return (row_potential, col_potential)


def solution(mesh):
    placed = (P(("row", "col"), None), P(("col", "row"), None), P())
    return jax.shard_map(
        per_device, mesh=mesh, in_specs=placed, out_specs=(P("row"), P("col")), check_vma=False
    )
```

profile of v0, /device:TPU:0, one launch (start us, length us, event | category | flops | bytes accessed | tf_op | source)
XLA Modules:
  0.0 548.1 jit_solution(1671525743373473632)
XLA Ops:
  7.2 0.0 all-gather.3.cloned.1.call-start
  7.2 0.7 all-gather.3.cloned.1.call-update
  7.9 0.0 all-gather.5.cloned.1.call-start
  7.9 0.7 all-gather.5.cloned.1.call-update
  9.3 25.6 %all-gather.3.cloned.1.call-done = f32[2048,256]{1,0:T(8,128)} async-done(((f32[512,256]{1,0:T(8,128)}), f32[2048,256]{1,0:T(8,128)}) %all-gather.3.cloned.1.call-update) | async-done | bytes 2097168 | tf_op jit(solution)/shard_map/all_gather | solution.py:42
  34.9 1.9 multiply_reduce_fusion.1
  36.8 73.6 %all-gather.5.cloned.1.call-done = f32[4096,256]{1,0:T(8,128)} async-done(((f32[512,256]{1,0:T(8,128)}), f32[4096,256]{1,0:T(8,128)}) %all-gather.5.cloned.1.call-update) | async-done | bytes 4194320 | tf_op jit(solution)/shard_map/all_gather | solution.py:43
  110.4 2.8 multiply_reduce_fusion
  113.2 38.7 %fusion = (f32[2048]{0:T(1024)S(1)}, f32[2048,4096]{1,0:T(8,128)}) fusion(f32[]{:T(128)} %bitcast, f32[2048,256]{1,0:T(8,128)} %all-gather.3.cloned.1.call-done, f32[4096,256]{1,0:T(8,128)} %all-gather.5.cloned.1.call-done, f32[4096]{0:T(1024)S(1)} %multiply_reduce_fusion, f32[2048]{0:T(1024)S(1)} %multiply_reduce_fusion.1), kind=kOutput, calls=%fused_computation.13 | convolution fusion | flops 25820133376 | bytes 39878660 | tf_op jit(solution)/shard_map/dot_general | solution.py:14
  152.0 5.7 %pmax.42 = f32[2048]{0:T(1024)S(1)} all-reduce(f32[2048]{0:T(1024)S(1)} %get-tuple-element.2), channel_id=1, replica_groups=mesh['row'=8,'col'=4] {'col'}, use_global_device_ids=true, to_apply=%region_3.0 | all-reduce | flops 2048 | bytes 16384 | tf_op jit(solution)/shard_map/pmax | solution.py:25
  157.7 14.5 %exponential_reduce_fusion.5 = f32[2048]{0:T(1024)S(1)} fusion(f32[2048]{0:T(1024)S(1)} %pmax.42, f32[]{:T(128)} %bitcast, f32[2048,4096]{1,0:T(8,128)} %get-tuple-element.3), kind=kLoop, calls=%fused_computation.10 | loop fusion | flops 33552384 | bytes 33570820 | tf_op jit(solution)/shard_map/reduce_sum | solution.py:26
  172.2 6.9 %psum.42 = f32[2048]{0:T(1024)S(1)} all-reduce(f32[2048]{0:T(1024)S(1)} %exponential_reduce_fusion.5), channel_id=1, replica_groups=mesh['row'=8,'col'=4] {'col'}, use_global_device_ids=true, to_apply=%region_5.0 | all-reduce | flops 2048 | bytes 16384 | tf_op jit(solution)/shard_map/psum | solution.py:26
  179.1 13.1 %fusion.3 = f32[4096]{0:T(1024)S(1)} fusion(f32[]{:T(128)} %bitcast, f32[2048,4096]{1,0:T(8,128)} %get-tuple-element.3, f32[2048]{0:T(1024)S(1)} %multiply_subtract_fusion.6), kind=kLoop, calls=%fused_computation.17 | loop fusion | flops 25161728 | bytes 33579012 | tf_op jit(solution)/shard_map/reduce_max | solution.py:31
  192.3 35.0 %pmax.43 = f32[4096]{0:T(1024)S(1)} all-reduce(f32[4096]{0:T(1024)S(1)} %fusion.3), channel_id=1, replica_groups=mesh['row'=8,'col'=4] {'row'}, use_global_device_ids=true, to_apply=%region_7.0 | all-reduce | flops 4096 | bytes 32768 | tf_op jit(solution)/shard_map/pmax | solution.py:31
  227.3 14.4 %exponential_reduce_fusion.4 = f32[4096]{0:T(1024)S(1)} fusion(f32[4096]{0:T(1024)S(1)} %pmax.43, f32[]{:T(128)} %bitcast, f32[2048,4096]{1,0:T(8,128)} %get-tuple-element.3, f32[2048]{0:T(1024)S(1)} %multiply_subtract_fusion.6), kind=kLoop, calls=%fused_computation.8 | loop fusion | flops 33550336 | bytes 33595396 | tf_op jit(solution)/shard_map/reduce_sum | solution.py:32
  241.7 33.0 %psum.43 = f32[4096]{0:T(1024)S(1)} all-reduce(f32[4096]{0:T(1024)S(1)} %exponential_reduce_fusion.4), channel_id=1, replica_groups=mesh['row'=8,'col'=4] {'row'}, use_global_device_ids=true, to_apply=%region_9.0 | all-reduce | flops 4096 | bytes 32768 | tf_op jit(solution)/shard_map/psum | solution.py:32
  274.7 12.8 %fusion.1 = f32[2048]{0:T(1024)S(1)} fusion(f32[]{:T(128)} %bitcast, f32[2048,4096]{1,0:T(8,128)} %get-tuple-element.3, f32[4096]{0:T(1024)S(1)} %multiply_subtract_fusion.3), kind=kLoop, calls=%fused_computation.14 | loop fusion | flops 25163776 | bytes 33579012 | tf_op jit(solution)/shard_map/reduce_max | solution.py:25
  287.4 5.9 %pmax.44 = f32[2048]{0:T(1024)S(1)} all-reduce(f32[2048]{0:T(1024)S(1)} %fusion.1), channel_id=1, replica_groups=mesh['row'=8,'col'=4] {'col'}, use_global_device_ids=true, to_apply=%region_11.0 | all-reduce | flops 2048 | bytes 16384 | tf_op jit(solution)/shard_map/pmax | solution.py:25
  293.3 14.6 %exponential_reduce_fusion.3 = f32[2048]{0:T(1024)S(1)} fusion(f32[2048]{0:T(1024)S(1)} %pmax.44, f32[]{:T(128)} %bitcast, f32[2048,4096]{1,0:T(8,128)} %get-tuple-element.3, f32[4096]{0:T(1024)S(1)} %multiply_subtract_fusion.3), kind=kLoop, calls=%fused_computation.6 | loop fusion | flops 33552384 | bytes 33587204 | tf_op jit(solution)/shard_map/reduce_sum | solution.py:26
  307.9 5.9 %psum.44 = f32[2048]{0:T(1024)S(1)} all-reduce(f32[2048]{0:T(1024)S(1)} %exponential_reduce_fusion.3), channel_id=1, replica_groups=mesh['row'=8,'col'=4] {'col'}, use_global_device_ids=true, to_apply=%region_13.0 | all-reduce | flops 2048 | bytes 16384 | tf_op jit(solution)/shard_map/psum | solution.py:26
  313.8 13.1 %fusion.4 = f32[4096]{0:T(1024)S(1)} fusion(f32[]{:T(128)} %bitcast, f32[2048,4096]{1,0:T(8,128)} %get-tuple-element.3, f32[2048]{0:T(1024)S(1)} %multiply_subtract_fusion.5), kind=kLoop, calls=%fused_computation.18 | loop fusion | flops 25161728 | bytes 33579012 | tf_op jit(solution)/shard_map/reduce_max | solution.py:31
  326.9 33.0 %pmax.45 = f32[4096]{0:T(1024)S(1)} all-reduce(f32[4096]{0:T(1024)S(1)} %fusion.4), channel_id=1, replica_groups=mesh['row'=8,'col'=4] {'row'}, use_global_device_ids=true, to_apply=%region_15.0 | all-reduce | flops 4096 | bytes 32768 | tf_op jit(solution)/shard_map/pmax | solution.py:31
  359.9 14.4 %exponential_reduce_fusion.2 = f32[4096]{0:T(1024)S(1)} fusion(f32[4096]{0:T(1024)S(1)} %pmax.45, f32[]{:T(128)} %bitcast, f32[2048,4096]{1,0:T(8,128)} %get-tuple-element.3, f32[2048]{0:T(1024)S(1)} %multiply_subtract_fusion.5), kind=kLoop, calls=%fused_computation.4 | loop fusion | flops 33550336 | bytes 33595396 | tf_op jit(solution)/shard_map/reduce_sum | solution.py:32
  374.3 33.0 %psum.45 = f32[4096]{0:T(1024)S(1)} all-reduce(f32[4096]{0:T(1024)S(1)} %exponential_reduce_fusion.2), channel_id=1, replica_groups=mesh['row'=8,'col'=4] {'row'}, use_global_device_ids=true, to_apply=%region_17.0 | all-reduce | flops 4096 | bytes 32768 | tf_op jit(solution)/shard_map/psum | solution.py:32
  407.3 12.8 %fusion.2 = f32[2048]{0:T(1024)S(1)} fusion(f32[]{:T(128)} %bitcast, f32[2048,4096]{1,0:T(8,128)} %get-tuple-element.3, f32[4096]{0:T(1024)S(1)} %multiply_subtract_fusion.2), kind=kLoop, calls=%fused_computation.15 | loop fusion | flops 25163776 | bytes 33579012 | tf_op jit(solution)/shard_map/reduce_max | solution.py:25
  420.0 5.8 %pmax.46 = f32[2048]{0:T(1024)S(1)} all-reduce(f32[2048]{0:T(1024)S(1)} %fusion.2), channel_id=1, replica_groups=mesh['row'=8,'col'=4] {'col'}, use_global_device_ids=true, to_apply=%region_19.0 | all-reduce | flops 2048 | bytes 16384 | tf_op jit(solution)/shard_map/pmax | solution.py:25
  425.8 14.6 %exponential_reduce_fusion.1 = f32[2048]{0:T(1024)S(1)} fusion(f32[2048]{0:T(1024)S(1)} %pmax.46, f32[]{:T(128)} %bitcast, f32[2048,4096]{1,0:T(8,128)} %get-tuple-element.3, f32[4096]{0:T(1024)S(1)} %multiply_subtract_fusion.2), kind=kLoop, calls=%fused_computation.2 | loop fusion | flops 33552384 | bytes 33587204 | tf_op jit(solution)/shard_map/reduce_sum | solution.py:26
  440.4 6.8 %psum.46 = f32[2048]{0:T(1024)S(1)} all-reduce(f32[2048]{0:T(1024)S(1)} %exponential_reduce_fusion.1), channel_id=1, replica_groups=mesh['row'=8,'col'=4] {'col'}, use_global_device_ids=true, to_apply=%region_21.0 | all-reduce | flops 2048 | bytes 16384 | tf_op jit(solution)/shard_map/psum | solution.py:26
  447.2 0.0 copy-start
  447.2 13.1 %fusion.5 = f32[4096]{0:T(1024)S(1)} fusion(f32[]{:T(128)} %bitcast, f32[2048,4096]{1,0:T(8,128)} %get-tuple-element.3, f32[2048]{0:T(1024)S(1)} %multiply_subtract_fusion.4), kind=kLoop, calls=%fused_computation.19 | loop fusion | flops 25161728 | bytes 33579012 | tf_op jit(solution)/shard_map/reduce_max | solution.py:31
  460.3 33.0 %pmax.47 = f32[4096]{0:T(1024)S(1)} all-reduce(f32[4096]{0:T(1024)S(1)} %fusion.5), channel_id=1, replica_groups=mesh['row'=8,'col'=4] {'row'}, use_global_device_ids=true, to_apply=%region_23.0 | all-reduce | flops 4096 | bytes 32768 | tf_op jit(solution)/shard_map/pmax | solution.py:31
  493.3 14.4 %exponential_reduce_fusion = f32[4096]{0:T(1024)S(1)} fusion(f32[4096]{0:T(1024)S(1)} %pmax.47, f32[]{:T(128)} %bitcast, f32[2048,4096]{1,0:T(8,128)} %get-tuple-element.3, f32[2048]{0:T(1024)S(1)} %multiply_subtract_fusion.4), kind=kLoop, calls=%fused_computation | loop fusion | flops 33550336 | bytes 33595396 | tf_op jit(solution)/shard_map/reduce_sum | solution.py:32
  507.7 0.0 copy-done
  507.7 33.0 %psum.47 = f32[4096]{0:T(1024)S(1)} all-reduce(f32[4096]{0:T(1024)S(1)} %exponential_reduce_fusion), channel_id=1, replica_groups=mesh['row'=8,'col'=4] {'row'}, use_global_device_ids=true, to_apply=%region_25.0 | all-reduce | flops 4096 | bytes 32768 | tf_op jit(solution)/shard_map/psum | solution.py:32
  540.7 0.6 multiply_subtract_fusion.1
  (5 shorter events, 0.1 us)
Async XLA Ops:
  7.2 27.7 %all-gather.3.cloned.1.call-start = ((), (), s32[]{:S(2)}) async-start(), calls=%async_computation | async-start | bytes 2621440 | tf_op jit(solution)/shard_map/all_gather | solution.py:42
  7.9 102.5 %all-gather.5.cloned.1.call-start = ((), (), s32[]{:S(2)}) async-start(), calls=%async_computation.1 | async-start | bytes 4718592 | tf_op jit(solution)/shard_map/all_gather | solution.py:43
  447.2 60.5 %copy-start = (f32[2048]{0:T(1024)}, f32[2048]{0:T(1024)S(1)}, u32[]{:S(2)}) copy-start(f32[2048]{0:T(1024)S(1)} %multiply_subtract_fusion.4) | copy-start | bytes 24580
Sparse Core Ops, SparseCore 0:
  9.6 25.2 all-gather.2
  37.0 73.3 all-gather.4
where the time goes:
time: 550 us; the launch traced here: 548 us
  blocking collectives  237 us (43%)
  other arithmetic  157 us (29%)
  waiting for transfers between devices  101 us (18%)
  matrix products  38.7 us (7%)
  between operations  14.9 us (3%)
    pmax x3, blocking collectives, logsum_row(): peak = lax.pmax(jnp.max(scores, axis=0), 'row')  101 us
    psum x3, blocking collectives, logsum_row(): totals = lax.psum(jnp.sum(jnp.exp(scores - peak[None, :]), axis=0), 'row')  98.9 us
    all_gather x1, waiting for transfers between devices, per_device(): lax.all_gather(passages, 'row', axis=0, tiled=True)  73.6 us
    reduce_sum x3, other arithmetic, logsum_col(): totals = lax.psum(jnp.sum(jnp.exp(scores - peak[:, None]), axis=1), 'col')  43.7 us
    reduce_sum x3, other arithmetic, logsum_row(): totals = lax.psum(jnp.sum(jnp.exp(scores - peak[None, :]), axis=0), 'row')  43.1 us
    reduce_max x3, other arithmetic, logsum_row(): peak = lax.pmax(jnp.max(scores, axis=0), 'row')  39.4 us
    dot_general x1, matrix products, inner_costs(): lax.dot_general(left, right, (((1,), (1,)), ((), ())), precision=lax.Prec...  38.7 us
    all_gather x1, waiting for transfers between devices, per_device(): query_block = lax.all_gather(queries, 'col', axis=0, tiled=True)  25.6 us
  transfers between devices with their start and end apart: 2, of which 2 were waited for; matrix products, arithmetic and copies ran while one was open for 0% of the time, Pallas kernels for 0%

commit v1 on v0

v1 whole, which is shorter than its diff:
```python
import functools
import math

import jax
import jax.numpy as jnp
from jax import lax
from jax.experimental import pallas as pl
from jax.experimental.pallas import tpu as pltpu
from jax.sharding import PartitionSpec as P

ITERS = 3
LOG2E = 1.4426950408889634
LOW = -3.0e38
LANES = 128
MESH = pl.DeviceIdType.MESH


def tree(op, values):
    values = list(values)
    while len(values) > 1:
        values = [
            op(values[i], values[i + 1]) if i + 1 < len(values) else values[i]
            for i in range(0, len(values), 2)
        ]
    return values[0]


def online(m, s, z):
    new = jnp.maximum(m, tree(jnp.maximum, z))
    return new, s * jnp.exp2(m - new) + tree(jnp.add, [jnp.exp2(v - new) for v in z])


def kernel(
    nr, nc, log_q, log_p,
    mc_ref, q_ref, p_ref, f_out, g_out,
    tile, qbuf, pbuf, q3, p3, qn, pn, g8, fb, m_rows, s_rows, m_cols, s_cols, rbuf, cbuf,
    q_send, q_recv, p_send, p_recv, r_send, r_recv, c_send, c_recv,
):
    row, col = lax.axis_index("row"), lax.axis_index("col")
    qb, depth = q_ref.shape
    pb = p_ref.shape[0]
    rows, cols = qb * nc, pb * nr
    nx = nc // 2
    core = lax.rem(col, 2)
    sibling = col + 1 - 2 * core

    barrier = pltpu.get_barrier_semaphore()
    for d in range(1, nr):
        pl.semaphore_signal(
            barrier, inc=1, device_id=(lax.rem(row + d, nr), col), device_id_type=MESH
        )
    for d in range(1, nc):
        pl.semaphore_signal(
            barrier, inc=1, device_id=(row, lax.rem(col + d, nc)), device_id_type=MESH
        )
    pl.semaphore_wait(barrier, nr + nc - 2)

    def remote(src, dst, send, recv, device):
        return pltpu.make_async_remote_copy(
            src_ref=src, dst_ref=dst, send_sem=send, recv_sem=recv,
            device_id=device, device_id_type=MESH,
        )

    half = nr // 2

    def at(pos):
        pos = lax.rem(pos + 2 * nr, nr)
        y = pos // half
        z = pos * (1 - y) + (nr - 1 - pos) * y
        return 2 * z + y

    row_y = lax.rem(row, 2)
    row_z = row // 2
    pos = row_z + row_y * (nr - 1 - 2 * row_z)
    ahead, behind = at(pos + 1), at(pos - 1)

    def ring(step):
        a, b = at(pos - (step - 1)), at(pos + (step - 1))
        if step == half:
            h = pb // 2
            parts = (pl.ds(0, h), pl.ds(h, h))
        else:
            parts = (pl.ds(0, pb), pl.ds(0, pb))
        out = []
        for way, (owner, device) in enumerate(((a, ahead), (b, behind))):
            src = p_ref.at[parts[way]] if step == 1 else pbuf.at[owner, parts[way]]
            out.append(
                remote(
                    src, pbuf.at[owner, parts[way]],
                    p_send.at[way, step], p_recv.at[way, step], (device, col),
                )
            )
        return out

    steps = {1: ring(1)}
    for c in steps[1]:
        c.start()

    cross, passed = [], []
    for d in range(1, nx):
        cross.append(
            remote(
                q_ref, qbuf.at[col], q_send.at[d], q_recv.at[d],
                (row, lax.rem(col + 2 * d, nc)),
            )
        )
    for c in cross:
        c.start()
    own = remote(q_ref, qbuf.at[col], q_send.at[0], q_recv.at[0], (row, sibling))
    own.start()

    kappa = (10.0 * LOG2E) / jnp.full((8, LANES), mc_ref[0], jnp.float32)
    kappa1 = kappa[0:1, :]

    def norms(x):
        sq = x * x
        total = sq[:, 0:LANES]
        for k in range(1, depth // LANES):
            total = total + sq[:, k * LANES : (k + 1) * LANES]
        return jnp.sum(total.T, axis=0, keepdims=True)

    def split_q(block, ref):
        def body(i, _):
            x = ref[pl.ds(pl.multiple_of(i * LANES, LANES), LANES), :]
            qn[block, pl.ds(i, 1), :] = norms(x)
            for k in range(depth // LANES):
                v = x[:, k * LANES : (k + 1) * LANES] * (2.0 * kappa1)
                hi = v.astype(jnp.bfloat16)
                lo = (v - hi.astype(jnp.float32)).astype(jnp.bfloat16)
                at_row = pl.ds(pl.multiple_of(block * qb + i * LANES, LANES), LANES)
                q3[at_row, k * LANES : (k + 1) * LANES] = hi
                q3[at_row, depth + k * LANES : depth + (k + 1) * LANES] = hi
                q3[at_row, 2 * depth + k * LANES : 2 * depth + (k + 1) * LANES] = lo
            return 0

        lax.fori_loop(0, qb // LANES, body, 0)

    m_rows[...] = jnp.full(m_rows.shape, LOW, jnp.float32)
    s_rows[...] = jnp.zeros(s_rows.shape, jnp.float32)

    def work(block, ref, start, size):
        base = pl.multiple_of(block * pb + start, LANES)
        for i in range(size // LANES):
            at_row = start + i * LANES
            x = ref[at_row : at_row + LANES, :]
            norm = norms(x)
            pn[block, start // LANES + i : start // LANES + i + 1, :] = norm
            g8[:, pl.ds(pl.multiple_of(base + i * LANES, LANES), LANES)] = jnp.broadcast_to(
                -norm * kappa1, (8, LANES)
            )
            hi = x.astype(jnp.bfloat16)
            lo = (x - hi.astype(jnp.float32)).astype(jnp.bfloat16)
            p3[i * LANES : (i + 1) * LANES, 0:depth] = hi
            p3[i * LANES : (i + 1) * LANES, depth : 2 * depth] = lo
            p3[i * LANES : (i + 1) * LANES, 2 * depth : 3 * depth] = hi

        def product(i, _):
            at_row = pl.ds(pl.multiple_of(i * 512, 512), 512)
            tile[at_row, pl.ds(base, size)] = lax.dot_general(
                q3[at_row, :], p3[0:size, :], (((1,), (1,)), ((), ())),
                preferred_element_type=jnp.float32,
            )
            return 0

        lax.fori_loop(0, rows // 512, product, 0)
        width = size // LANES

        def first(i, _):
            g = [g8[:, pl.ds(pl.multiple_of(base + k * LANES, LANES), LANES)] for k in range(width)]
            for r in range(8):
                at_row = pl.ds(pl.multiple_of(i * 64 + r * 8, 8), 8)
                z = [
                    tile[at_row, pl.ds(pl.multiple_of(base + k * LANES, LANES), LANES)] + g[k]
                    for k in range(width)
                ]
                m_rows[at_row, :], s_rows[at_row, :] = online(m_rows[at_row, :], s_rows[at_row, :], z)
            return 0

        lax.fori_loop(0, rows // 64, first, 0)

    split_q(col, q_ref)
    for d, c in enumerate(cross, 1):
        c.wait_recv()
        source = lax.rem(col - 2 * d + nc, nc)
        fwd = remote(
            qbuf.at[source], qbuf.at[source], q_send.at[nx + d - 1], q_recv.at[nx + d - 1],
            (row, sibling),
        )
        fwd.start()
        passed.append(fwd)
        split_q(source, qbuf.at[source])
    own.wait_recv()
    split_q(sibling, qbuf.at[sibling])
    for d, c in enumerate(passed, 1):
        c.wait_recv()
        source = lax.rem(sibling - 2 * d + nc, nc)
        split_q(source, qbuf.at[source])

    for step in range(1, half + 1):
        if step == 1:
            work(row, p_ref, 0, pb)
        for c in steps[step]:
            c.wait_recv()
        if step < half:
            steps[step + 1] = ring(step + 1)
            for c in steps[step + 1]:
                c.start()
            for owner in (at(pos - step), at(pos + step)):
                work(owner, pbuf.at[owner], 0, pb)
        else:
            owner = at(pos + half)
            work(owner, pbuf.at[owner], 0, pb)

    def exchange(buf, t, me, n, send, recv, device):
        sent = []
        for d in range(1, n):
            c = remote(
                buf.at[t, me], buf.at[t, me], send.at[t, d], recv.at[t, d],
                device(lax.rem(me + d, n)),
            )
            c.start()
            sent.append(c)
        for c in sent:
            c.wait_recv()
        parts = [buf[t, i] for i in range(n)]
        peak = tree(jnp.maximum, parts)
        total = jnp.exp2(parts[0] - peak)
        for part in parts[1:]:
            total = total + jnp.exp2(part - peak)
        for c in sent:
            c.wait_send()
        return peak + jnp.log2(total)

    def row_pass():
        wide = cols // LANES
        chunk = min(16, wide)

        def body(i, _):
            pair = []
            for h in range(2):
                pair.append(
                    (jnp.full((8, LANES), LOW, jnp.float32), jnp.zeros((8, LANES), jnp.float32))
                )
            for k0 in range(0, wide, chunk):
                for h in range(2):
                    at_row = pl.ds(pl.multiple_of(i * 16 + h * 8, 8), 8)
                    z = [
                        tile[at_row, k * LANES : (k + 1) * LANES] + g8[:, k * LANES : (k + 1) * LANES]
                        for k in range(k0, k0 + chunk)
                    ]
                    pair[h] = online(*pair[h], z)
            for h in range(2):
                at_row = pl.ds(pl.multiple_of(i * 16 + h * 8, 8), 8)
                m_rows[at_row, :], s_rows[at_row, :] = pair[h]
            return 0

        lax.fori_loop(0, rows // 16, body, 0)

    def col_pass():
        def strip(k, _):
            lanes = [
                pl.ds(pl.multiple_of(k * 2 * LANES + h * LANES, LANES), LANES) for h in range(2)
            ]

            def body(c, carry):
                f = [fb[pl.ds(pl.multiple_of(c * 128 + r * 8, 8), 8), :] for r in range(16)]
                out = []
                for h in range(2):
                    z = [
                        tile[pl.ds(pl.multiple_of(c * 128 + r * 8, 8), 8), lanes[h]] + f[r]
                        for r in range(16)
                    ]
                    out.extend(online(carry[2 * h], carry[2 * h + 1], z))
                return tuple(out)

            low = jnp.full((8, LANES), LOW, jnp.float32)
            zero = jnp.zeros((8, LANES), jnp.float32)
            done = lax.fori_loop(0, rows // 128, body, (low, zero, low, zero))
            for h in range(2):
                m_cols[:, lanes[h]] = done[2 * h]
                s_cols[:, lanes[h]] = done[2 * h + 1]
            return 0

        lax.fori_loop(0, cols // (2 * LANES), strip, 0)

    for t in range(ITERS):
        if t > 0:
            row_pass()
        for b in range(rows // LANES):
            here = slice(b * LANES, (b + 1) * LANES)
            m, s = m_rows[here, :].T, s_rows[here, :].T
            peak = jnp.max(m, axis=0, keepdims=True)
            total = jnp.sum(s * jnp.exp2(m - peak), axis=0, keepdims=True)
            rbuf[t, col, b : b + 1, :] = peak + jnp.log2(total)
        f = -log_q - exchange(rbuf, t, col, nc, r_send, r_recv, lambda i: (row, i))
        for b in range(rows // LANES):
            fb[b * LANES : (b + 1) * LANES, :] = jnp.broadcast_to(
                f[b : b + 1, :], (LANES, LANES)
            ).T
        if t == ITERS - 1:
            per = qb // LANES
            for b in range(nc):
                here = slice(b * per, (b + 1) * per)
                f_out[here, :] = f[here, :] / kappa1 + qn[b]
        col_pass()
        for k in range(cols // LANES):
            here = slice(k * LANES, (k + 1) * LANES)
            m, s = m_cols[:, here], s_cols[:, here]
            peak = jnp.max(m, axis=0, keepdims=True)
            total = jnp.sum(s * jnp.exp2(m - peak), axis=0, keepdims=True)
            cbuf[t, row, k : k + 1, :] = peak + jnp.log2(total)
        g = -log_p - exchange(cbuf, t, row, nr, c_send, c_recv, lambda i: (i, col))
        if t < ITERS - 1:
            for k in range(cols // LANES):
                g8[:, k * LANES : (k + 1) * LANES] = jnp.broadcast_to(g[k : k + 1, :], (8, LANES))
        else:
            per = pb // LANES
            for b in range(nr):
                here = slice(b * per, (b + 1) * per)
                g_out[here, :] = g[here, :] / kappa1 + pn[b]

    for c in cross + [own] + passed:
        c.wait_send()
    for step in range(1, half + 1):
        for c in steps[step]:
            c.wait_send()


def per_device(nr, nc, queries, passages, mean_cost):
    qb, depth = queries.shape
    pb = passages.shape[0]
    rows, cols = qb * nc, pb * nr
    f32, bf16 = jnp.float32, jnp.bfloat16
    dma = pltpu.SemaphoreType.DMA
    vmem = pl.BlockSpec(memory_space=pltpu.VMEM)
    f, g = pl.pallas_call(
        functools.partial(
            kernel, nr, nc, math.log2(qb * nr * nc), math.log2(pb * nr * nc)
        ),
        out_shape=(
            jax.ShapeDtypeStruct((rows // LANES, LANES), f32),
            jax.ShapeDtypeStruct((cols // LANES, LANES), f32),
        ),
        in_specs=[pl.BlockSpec(memory_space=pltpu.SMEM), vmem, vmem],
        out_specs=(vmem, vmem),
        scratch_shapes=[
            pltpu.VMEM((rows, cols), f32),
            pltpu.VMEM((nc, qb, depth), f32),
            pltpu.VMEM((nr, pb, depth), f32),
            pltpu.VMEM((rows, 3 * depth), bf16),
            pltpu.VMEM((pb, 3 * depth), bf16),
            pltpu.VMEM((nc, qb // LANES, LANES), f32),
            pltpu.VMEM((nr, pb // LANES, LANES), f32),
            pltpu.VMEM((8, cols), f32),
            pltpu.VMEM((rows, LANES), f32),
            pltpu.VMEM((rows, LANES), f32),
            pltpu.VMEM((rows, LANES), f32),
            pltpu.VMEM((8, cols), f32),
            pltpu.VMEM((8, cols), f32),
            pltpu.VMEM((ITERS, nc, rows // LANES, LANES), f32),
            pltpu.VMEM((ITERS, nr, cols // LANES, LANES), f32),
            dma((nc,)), dma((nc,)),
            dma((2, nr // 2 + 1)), dma((2, nr // 2 + 1)),
            dma((ITERS, nc)), dma((ITERS, nc)),
            dma((ITERS, nr)), dma((ITERS, nr)),
        ],
        compiler_params=pltpu.CompilerParams(
            collective_id=0, has_side_effects=True, vmem_limit_bytes=60 * 1024 * 1024
        ),
        cost_estimate=pl.CostEstimate(
            flops=6 * rows * cols * depth,
            bytes_accessed=4 * depth * (qb + pb),
            transcendentals=2 * ITERS * rows * cols,
        ),
    )(mean_cost, queries, passages)
    return f.reshape(rows), g.reshape(cols)


def solution(mesh):
    nr, nc = mesh.shape["row"], mesh.shape["col"]
    placed = (P(("row", "col"), None), P(("col", "row"), None), P())
    return jax.shard_map(
        functools.partial(per_device, nr, nc),
        mesh=mesh, in_specs=placed, out_specs=(P("row"), P("col")), check_vma=False,
    )
```

time: 550 us -> 169 us (0.31)
  blocking collectives: 237 us -> 0 us
  Pallas kernels: 0 us -> 166 us
  other arithmetic: 157 us -> 0 us
  waiting for transfers between devices: 101 us -> 0 us
  matrix products: 38.7 us -> 0 us
  between operations: 14.9 us -> 1.29 us
    pallas_call x0 -> x1, Pallas kernels: none -> 166 us  [per_device(): pl.pallas_call(functools.partial(kernel, nr, nc, math.log2(qb * nr * nc),...]
    psum x6 -> x0, blocking collectives: 118 us -> none  [the longest x3 98.9 us: logsum_row(): totals = lax.psum(jnp.sum(jnp.exp(scores - peak[None, :]), axis=0), 'row')]
    pmax x6 -> x0, blocking collectives: 118 us -> none  [the longest x3 101 us: logsum_row(): peak = lax.pmax(jnp.max(scores, axis=0), 'row')]
    all_gather x2 -> x0, waiting for transfers between devices: 99.2 us -> none  [the longest x1 73.6 us: per_device(): lax.all_gather(passages, 'row', axis=0, tiled=True)]
    reduce_sum x8 -> x0, other arithmetic: 91.5 us -> none  [the longest x3 43.7 us: logsum_col(): totals = lax.psum(jnp.sum(jnp.exp(scores - peak[:, None]), axis=1), 'col')]
    reduce_max x5 -> x0, other arithmetic: 64.9 us -> none  [the longest x3 39.4 us: logsum_row(): peak = lax.pmax(jnp.max(scores, axis=0), 'row')]
    dot_general x1 -> x0, matrix products: 38.7 us -> none  [inner_costs(): lax.dot_general(left, right, (((1,), (1,)), ((), ())), precision=lax.Prec...]
  transfers between devices with their start and end apart: 2 -> 0, of which waited for: 2 -> 0; matrix products, arithmetic and copies ran while one was open for 0% -> 0% of each run, Pallas kernels for 0% -> 0%
where the time goes in v1:
time: 169 us
  Pallas kernels  166 us (98%)
  local copies, waits for them, and re-layouts  1.91 us (1%)
    pallas_call x1, Pallas kernels, per_device(): pl.pallas_call(functools.partial(kernel, nr, nc, math.log2(qb * nr * nc),...  166 us

profile of v1, /device:TPU:0, one launch (start us, length us, event | category | flops | bytes accessed | tf_op | source)
XLA Modules:
  0.0 168.8 jit_solution(17061845466993249432)
XLA Ops:
  1.3 165.6 %shard_map.50 = (f32[16,128]{1,0:T(8,128)}, f32[32,128]{1,0:T(8,128)}) custom-call(f32[1]{0:T(128)S(6)} %copy.7.mc_ref, f32[512,256]{1,0:T(8,128)} %q_ref.1, f32[512,256]{1,0:T(8,128)} %p_ref.1), custom_call_target="tpu_custom_call" | custom-call | flops 12884901888 | bytes 1048576 | tf_op jit(solution)/shard_map/pallas_call | solution.py:336
  166.9 0.0 copy-start
  166.9 1.3 copy.8
  168.2 0.0 copy-done
  168.2 0.6 copy.9
Async XLA Ops:
  166.9 1.3 copy-start

commit v2 on v1

--- a/solution.py
+++ b/solution.py
@@ -138,13 +138,14 @@
     m_rows[...] = jnp.full(m_rows.shape, LOW, jnp.float32)
     s_rows[...] = jnp.zeros(s_rows.shape, jnp.float32)
 
-    def work(block, ref, start, size):
-        base = pl.multiple_of(block * pb + start, LANES)
-        for i in range(size // LANES):
-            at_row = start + i * LANES
-            x = ref[at_row : at_row + LANES, :]
+    wide = pb // LANES
+
+    def prepare(block, ref):
+        base = pl.multiple_of(block * pb, LANES)
+        for i in range(wide):
+            x = ref[i * LANES : (i + 1) * LANES, :]
             norm = norms(x)
-            pn[block, start // LANES + i : start // LANES + i + 1, :] = norm
+            pn[block, i : i + 1, :] = norm
             g8[:, pl.ds(pl.multiple_of(base + i * LANES, LANES), LANES)] = jnp.broadcast_to(
                 -norm * kappa1, (8, LANES)
             )
@@ -154,31 +155,152 @@
             p3[i * LANES : (i + 1) * LANES, depth : 2 * depth] = lo
             p3[i * LANES : (i + 1) * LANES, 2 * depth : 3 * depth] = hi
 
-        def product(i, _):
-            at_row = pl.ds(pl.multiple_of(i * 512, 512), 512)
-            tile[at_row, pl.ds(base, size)] = lax.dot_general(
-                q3[at_row, :], p3[0:size, :], (((1,), (1,)), ((), ())),
-                preferred_element_type=jnp.float32,
-            )
-            return 0
-
-        lax.fori_loop(0, rows // 512, product, 0)
-        width = size // LANES
+    def work(block, q_block):
+        base = pl.multiple_of(block * pb, LANES)
+        top = pl.multiple_of(q_block * qb, qb)
+        tile[pl.ds(top, qb), pl.ds(base, pb)] = lax.dot_general(
+            q3[pl.ds(top, qb), :], p3[...], (((1,), (1,)), ((), ())),
+            preferred_element_type=jnp.float32,
+        )
 
         def first(i, _):
-            g = [g8[:, pl.ds(pl.multiple_of(base + k * LANES, LANES), LANES)] for k in range(width)]
-            for r in range(8):
-                at_row = pl.ds(pl.multiple_of(i * 64 + r * 8, 8), 8)
+            g = [g8[:, pl.ds(pl.multiple_of(base + k * LANES, LANES), LANES)] for k in range(wide)]
+            for r in range(16):
+                at_row = pl.ds(pl.multiple_of(top + i * 128 + r * 8, 8), 8)
                 z = [
                     tile[at_row, pl.ds(pl.multiple_of(base + k * LANES, LANES), LANES)] + g[k]
-                    for k in range(width)
+                    for k in range(wide)
                 ]
                 m_rows[at_row, :], s_rows[at_row, :] = online(m_rows[at_row, :], s_rows[at_row, :], z)
             return 0
 
-        lax.fori_loop(0, rows // 64, first, 0)
-
+        lax.fori_loop(0, qb // 128, first, 0)
+
+    sent = []
+
+    def send_out(buf, t, h, me, n, send, recv, device):
+        size = buf.shape[2] // 2
+        half_part = buf.at[t, me, pl.ds(h * size, size)]
+        copies = []
+        for d in range(1, n):
+            c = remote(
+                half_part, half_part, send.at[t, h, d], recv.at[t, h, d], device(lax.rem(me + d, n))
+            )
+            c.start()
+            copies.append(c)
+        sent.extend(copies)
+        return copies
+
+    def take_in(buf, t, h, n, copies):
+        for c in copies:
+            c.wait_recv()
+        size = buf.shape[2] // 2
+        parts = [buf[t, i, h * size : (h + 1) * size, :] for i in range(n)]
+        peak = tree(jnp.maximum, parts)
+        total = jnp.exp2(parts[0] - peak)
+        for part in parts[1:]:
+            total = total + jnp.exp2(part - peak)
+        return peak + jnp.log2(total)
+
+    h_rows, h_cols = rows // 2, cols // 2
+
+    def send_rows(t, h):
+        for b in range(h * h_rows // LANES, (h + 1) * h_rows // LANES):
+            here = slice(b * LANES, (b + 1) * LANES)
+            m, s = m_rows[here, :].T, s_rows[here, :].T
+            peak = jnp.max(m, axis=0, keepdims=True)
+            total = jnp.sum(s * jnp.exp2(m - peak), axis=0, keepdims=True)
+            rbuf[t, col, b : b + 1, :] = peak + jnp.log2(total)
+        return send_out(rbuf, t, h, col, nc, r_send, r_recv, lambda i: (row, i))
+
+    def take_rows(t, h, copies):
+        f = -log_q - take_in(rbuf, t, h, nc, copies)
+        for b in range(h_rows // LANES):
+            at_row = h * h_rows + b * LANES
+            fb[at_row : at_row + LANES, :] = jnp.broadcast_to(f[b : b + 1, :], (LANES, LANES)).T
+        if t == ITERS - 1:
+            per = qb // LANES
+            for b in range(nc // 2):
+                block = h * (nc // 2) + b
+                f_out[block * per : (block + 1) * per, :] = (
+                    f[b * per : (b + 1) * per, :] / kappa1 + qn[block]
+                )
+
+    def send_cols(t, h):
+        for k in range(h * h_cols // LANES, (h + 1) * h_cols // LANES):
+            here = slice(k * LANES, (k + 1) * LANES)
+            m, s = m_cols[:, here], s_cols[:, here]
+            peak = jnp.max(m, axis=0, keepdims=True)
+            total = jnp.sum(s * jnp.exp2(m - peak), axis=0, keepdims=True)
+            cbuf[t, row, k : k + 1, :] = peak + jnp.log2(total)
+        return send_out(cbuf, t, h, row, nr, c_send, c_recv, lambda i: (i, col))
+
+    def take_cols(t, h, copies):
+        g = -log_p - take_in(cbuf, t, h, nr, copies)
+        if t < ITERS - 1:
+            for k in range(h_cols // LANES):
+                lane = h * h_cols + k * LANES
+                g8[:, lane : lane + LANES] = jnp.broadcast_to(g[k : k + 1, :], (8, LANES))
+        else:
+            per = pb // LANES
+            for b in range(nr // 2):
+                block = h * (nr // 2) + b
+                g_out[block * per : (block + 1) * per, :] = (
+                    g[b * per : (b + 1) * per, :] / kappa1 + pn[block]
+                )
+
+    low = jnp.full((8, LANES), LOW, jnp.float32)
+    zero = jnp.zeros((8, LANES), jnp.float32)
+
+    def row_pass(h, c):
+        def body(i, _):
+            spots = [pl.ds(pl.multiple_of(h * h_rows + i * 32 + r * 8, 8), 8) for r in range(4)]
+            pair = [(low, zero) if c == 0 else (m_rows[sp, :], s_rows[sp, :]) for sp in spots]
+            for k0 in range(c * h_cols // LANES, (c + 1) * h_cols // LANES, 16):
+                for r, at_row in enumerate(spots):
+                    z = [
+                        tile[at_row, k * LANES : (k + 1) * LANES] + g8[:, k * LANES : (k + 1) * LANES]
+                        for k in range(k0, k0 + 16)
+                    ]
+                    pair[r] = online(*pair[r], z)
+            for r, at_row in enumerate(spots):
+                m_rows[at_row, :], s_rows[at_row, :] = pair[r]
+            return 0
+
+        lax.fori_loop(0, h_rows // 32, body, 0, unroll=2)
+
+    def col_pass(h, c):
+        side = 4
+
+        def strip(k, _):
+            lanes = [
+                pl.ds(pl.multiple_of(c * h_cols + (k * side + i) * LANES, LANES), LANES)
+                for i in range(side)
+            ]
+
+            def body(j, carry):
+                spots = [pl.ds(pl.multiple_of(h * h_rows + j * 128 + r * 8, 8), 8) for r in range(16)]
+                f = [fb[sp, :] for sp in spots]
+                out = []
+                for i in range(side):
+                    z = [tile[sp, lanes[i]] + f[r] for r, sp in enumerate(spots)]
+                    out.append(online(*carry[i], z))
+                return tuple(out)
+
+            start = tuple((low, zero) if h == 0 else (m_cols[:, sp], s_cols[:, sp]) for sp in lanes)
+            done = lax.fori_loop(0, h_rows // 128, body, start, unroll=2)
+            for i in range(side):
+                m_cols[:, lanes[i]], s_cols[:, lanes[i]] = done[i]
+            return 0
+
+        lax.fori_loop(0, h_cols // (side * LANES), strip, 0)
+
+    prepare(row, p_ref)
     split_q(col, q_ref)
+    work(row, col)
+    own.wait_recv()
+    split_q(sibling, qbuf.at[sibling])
+    work(row, sibling)
     for d, c in enumerate(cross, 1):
         c.wait_recv()
         source = lax.rem(col - 2 * d + nc, nc)
@@ -188,137 +310,76 @@
         )
         fwd.start()
         passed.append(fwd)
+        if d == 1:
+            for r in steps[1]:
+                r.wait_recv()
+            steps[2] = ring(2)
+            for r in steps[2]:
+                r.start()
         split_q(source, qbuf.at[source])
-    own.wait_recv()
-    split_q(sibling, qbuf.at[sibling])
+        work(row, source)
     for d, c in enumerate(passed, 1):
         c.wait_recv()
         source = lax.rem(sibling - 2 * d + nc, nc)
         split_q(source, qbuf.at[source])
-
-    for step in range(1, half + 1):
-        if step == 1:
-            work(row, p_ref, 0, pb)
-        for c in steps[step]:
-            c.wait_recv()
-        if step < half:
+        work(row, source)
+
+    def all_queries(owner):
+        prepare(owner, pbuf.at[owner])
+
+        def body(i, _):
+            work(owner, i)
+            return 0
+
+        lax.fori_loop(0, nc, body, 0)
+
+    for step in range(1, half):
+        if step > 1:
+            for c in steps[step]:
+                c.wait_recv()
             steps[step + 1] = ring(step + 1)
             for c in steps[step + 1]:
                 c.start()
-            for owner in (at(pos - step), at(pos + step)):
-                work(owner, pbuf.at[owner], 0, pb)
-        else:
-            owner = at(pos + half)
-            work(owner, pbuf.at[owner], 0, pb)
-
-    def exchange(buf, t, me, n, send, recv, device):
-        sent = []
-        for d in range(1, n):
-            c = remote(
-                buf.at[t, me], buf.at[t, me], send.at[t, d], recv.at[t, d],
-                device(lax.rem(me + d, n)),
-            )
-            c.start()
-            sent.append(c)
-        for c in sent:
-            c.wait_recv()
-        parts = [buf[t, i] for i in range(n)]
-        peak = tree(jnp.maximum, parts)
-        total = jnp.exp2(parts[0] - peak)
-        for part in parts[1:]:
-            total = total + jnp.exp2(part - peak)
-        for c in sent:
-            c.wait_send()
-        return peak + jnp.log2(total)
-
-    def row_pass():
-        wide = cols // LANES
-        chunk = min(16, wide)
+        for owner in (at(pos - step), at(pos + step)):
+            all_queries(owner)
+    for c in steps[half]:
+        c.wait_recv()
+    owner = at(pos + half)
+    prepare(owner, pbuf.at[owner])
+    row_copies = []
+    for h in range(2):
 
         def body(i, _):
-            pair = []
-            for h in range(2):
-                pair.append(
-                    (jnp.full((8, LANES), LOW, jnp.float32), jnp.zeros((8, LANES), jnp.float32))
-                )
-            for k0 in range(0, wide, chunk):
-                for h in range(2):
-                    at_row = pl.ds(pl.multiple_of(i * 16 + h * 8, 8), 8)
-                    z = [
-                        tile[at_row, k * LANES : (k + 1) * LANES] + g8[:, k * LANES : (k + 1) * LANES]
-                        for k in range(k0, k0 + chunk)
-                    ]
-                    pair[h] = online(*pair[h], z)
-            for h in range(2):
-                at_row = pl.ds(pl.multiple_of(i * 16 + h * 8, 8), 8)
-                m_rows[at_row, :], s_rows[at_row, :] = pair[h]
-            return 0
-
-        lax.fori_loop(0, rows // 16, body, 0)
-
-    def col_pass():
-        def strip(k, _):
-            lanes = [
-                pl.ds(pl.multiple_of(k * 2 * LANES + h * LANES, LANES), LANES) for h in range(2)
-            ]
-
-            def body(c, carry):
-                f = [fb[pl.ds(pl.multiple_of(c * 128 + r * 8, 8), 8), :] for r in range(16)]
-                out = []
-                for h in range(2):
-                    z = [
-                        tile[pl.ds(pl.multiple_of(c * 128 + r * 8, 8), 8), lanes[h]] + f[r]
-                        for r in range(16)
-                    ]
-                    out.extend(online(carry[2 * h], carry[2 * h + 1], z))
-                return tuple(out)
-
-            low = jnp.full((8, LANES), LOW, jnp.float32)
-            zero = jnp.zeros((8, LANES), jnp.float32)
-            done = lax.fori_loop(0, rows // 128, body, (low, zero, low, zero))
-            for h in range(2):
-                m_cols[:, lanes[h]] = done[2 * h]
-                s_cols[:, lanes[h]] = done[2 * h + 1]
-            return 0
-
-        lax.fori_loop(0, cols // (2 * LANES), strip, 0)
+            work(owner, i)
+            return 0
+
+        lax.fori_loop(h * nc // 2, (h + 1) * nc // 2, body, 0)
+        row_copies.append(send_rows(0, h))
 
     for t in range(ITERS):
         if t > 0:
-            row_pass()
-        for b in range(rows // LANES):
-            here = slice(b * LANES, (b + 1) * LANES)
-            m, s = m_rows[here, :].T, s_rows[here, :].T
-            peak = jnp.max(m, axis=0, keepdims=True)
-            total = jnp.sum(s * jnp.exp2(m - peak), axis=0, keepdims=True)
-            rbuf[t, col, b : b + 1, :] = peak + jnp.log2(total)
-        f = -log_q - exchange(rbuf, t, col, nc, r_send, r_recv, lambda i: (row, i))
-        for b in range(rows // LANES):
-            fb[b * LANES : (b + 1) * LANES, :] = jnp.broadcast_to(
-                f[b : b + 1, :], (LANES, LANES)
-            ).T
-        if t == ITERS - 1:
-            per = qb // LANES
-            for b in range(nc):
-                here = slice(b * per, (b + 1) * per)
-                f_out[here, :] = f[here, :] / kappa1 + qn[b]
-        col_pass()
-        for k in range(cols // LANES):
-            here = slice(k * LANES, (k + 1) * LANES)
-            m, s = m_cols[:, here], s_cols[:, here]
-            peak = jnp.max(m, axis=0, keepdims=True)
-            total = jnp.sum(s * jnp.exp2(m - peak), axis=0, keepdims=True)
-            cbuf[t, row, k : k + 1, :] = peak + jnp.log2(total)
-        g = -log_p - exchange(cbuf, t, row, nr, c_send, c_recv, lambda i: (i, col))
-        if t < ITERS - 1:
-            for k in range(cols // LANES):
-                g8[:, k * LANES : (k + 1) * LANES] = jnp.broadcast_to(g[k : k + 1, :], (8, LANES))
-        else:
-            per = pb // LANES
-            for b in range(nr):
-                here = slice(b * per, (b + 1) * per)
-                g_out[here, :] = g[here, :] / kappa1 + pn[b]
-
+            row_copies = []
+            for h in range(2):
+                take_cols(t - 1, h, col_copies[h])
+                row_pass(0, h)
+                if h == 0:
+                    row_pass(1, 0)
+            row_copies.append(send_rows(t, 0))
+            row_pass(1, 1)
+            row_copies.append(send_rows(t, 1))
+        take_rows(t, 0, row_copies[0])
+        col_pass(0, 0)
+        col_pass(0, 1)
+        take_rows(t, 1, row_copies[1])
+        col_copies = []
+        for c in range(2):
+            col_pass(1, c)
+            col_copies.append(send_cols(t, c))
+    for h in range(2):
+        take_cols(ITERS - 1, h, col_copies[h])
+
+    for c in sent:
+        c.wait_send()
     for c in cross + [own] + passed:
         c.wait_send()
     for step in range(1, half + 1):
@@ -361,8 +422,8 @@
             pltpu.VMEM((ITERS, nr, cols // LANES, LANES), f32),
             dma((nc,)), dma((nc,)),
             dma((2, nr // 2 + 1)), dma((2, nr // 2 + 1)),
-            dma((ITERS, nc)), dma((ITERS, nc)),
-            dma((ITERS, nr)), dma((ITERS, nr)),
+            dma((ITERS, 2, nc)), dma((ITERS, 2, nc)),
+            dma((ITERS, 2, nr)), dma((ITERS, 2, nr)),
         ],
         compiler_params=pltpu.CompilerParams(
             collective_id=0, has_side_effects=True, vmem_limit_bytes=60 * 1024 * 1024

time: 169 us -> 128 us (0.76)
  Pallas kernels: 166 us -> 125 us
    pallas_call x1, Pallas kernels: 166 us -> 125 us  [per_device(): pl.pallas_call(functools.partial(kernel, nr, nc, math.log2(qb * nr * nc),...]
where the time goes in v2:
time: 128 us
  Pallas kernels  125 us (98%)
  local copies, waits for them, and re-layouts  1.91 us (1%)
  between operations  1.29 us (1%)
    pallas_call x1, Pallas kernels, per_device(): pl.pallas_call(functools.partial(kernel, nr, nc, math.log2(qb * nr * nc),...  125 us

profile of v2, /device:TPU:0, one launch (start us, length us, event | category | flops | bytes accessed | tf_op | source)
XLA Modules:
  0.0 128.1 jit_solution(18366366409107353104)
XLA Ops:
  1.3 124.9 %shard_map.50 = (f32[16,128]{1,0:T(8,128)}, f32[32,128]{1,0:T(8,128)}) custom-call(f32[1]{0:T(128)S(6)} %copy.7.mc_ref, f32[512,256]{1,0:T(8,128)} %q_ref.1, f32[512,256]{1,0:T(8,128)} %p_ref.1), custom_call_target="tpu_custom_call" | custom-call | flops 12884901888 | bytes 1048576 | tf_op jit(solution)/shard_map/pallas_call | solution.py:397
  126.2 0.0 copy-start
  126.2 1.3 %copy.8 = f32[2048]{0:T(1024)} copy(f32[2048]{0:T(1024)} %bitcast.3) | data formatting | bytes 16384
  127.5 0.0 copy-done
  127.5 0.6 copy.9
Async XLA Ops:
  126.2 1.3 %copy-start = (f32[32,128]{1,0:T(8,128)S(1)}, f32[32,128]{1,0:T(8,128)}, u32[]{:S(2)}) copy-start(f32[32,128]{1,0:T(8,128)} %get-tuple-element.5) | copy-start | bytes 49156

commit v3 on v2

--- a/solution.py
+++ b/solution.py
@@ -74,27 +74,31 @@
     pos = row_z + row_y * (nr - 1 - 2 * row_z)
     ahead, behind = at(pos + 1), at(pos - 1)
 
-    def ring(step):
-        a, b = at(pos - (step - 1)), at(pos + (step - 1))
-        if step == half:
-            h = pb // 2
-            parts = (pl.ds(0, h), pl.ds(h, h))
-        else:
-            parts = (pl.ds(0, pb), pl.ds(0, pb))
+    hb = pb // 2
+
+    def ring(step, turn):
         out = []
-        for way, (owner, device) in enumerate(((a, ahead), (b, behind))):
-            src = p_ref.at[parts[way]] if step == 1 else pbuf.at[owner, parts[way]]
-            out.append(
-                remote(
-                    src, pbuf.at[owner, parts[way]],
-                    p_send.at[way, step], p_recv.at[way, step], (device, col),
-                )
+        for way, device in enumerate((ahead, behind)):
+            owner = at(pos + (step - 1) * (2 * way - 1))
+            part = pl.ds((way + turn) % 2 * hb, hb)
+            src = p_ref.at[part] if step == 1 else pbuf.at[owner, part]
+            c = remote(
+                src, pbuf.at[owner, part],
+                p_send.at[way, step, turn], p_recv.at[way, step, turn], (device, col),
             )
+            c.start()
+            out.append(c)
         return out
 
-    steps = {1: ring(1)}
-    for c in steps[1]:
-        c.start()
+    steps = {}
+    for turn in range(2):
+        steps[1, turn] = ring(1, turn)
+
+    def pass_on(step, turn):
+        for c in steps[step, turn]:
+            c.wait_recv()
+        if step + 1 < half or (step + 1 == half and turn == 0):
+            steps[step + 1, turn] = ring(step + 1, turn)
 
     cross, passed = [], []
     for d in range(1, nx):
@@ -138,39 +142,44 @@
     m_rows[...] = jnp.full(m_rows.shape, LOW, jnp.float32)
     s_rows[...] = jnp.zeros(s_rows.shape, jnp.float32)
 
-    wide = pb // LANES
-
-    def prepare(block, ref):
-        base = pl.multiple_of(block * pb, LANES)
-        for i in range(wide):
-            x = ref[i * LANES : (i + 1) * LANES, :]
-            norm = norms(x)
-            pn[block, i : i + 1, :] = norm
-            g8[:, pl.ds(pl.multiple_of(base + i * LANES, LANES), LANES)] = jnp.broadcast_to(
-                -norm * kappa1, (8, LANES)
-            )
-            hi = x.astype(jnp.bfloat16)
-            lo = (x - hi.astype(jnp.float32)).astype(jnp.bfloat16)
-            p3[i * LANES : (i + 1) * LANES, 0:depth] = hi
-            p3[i * LANES : (i + 1) * LANES, depth : 2 * depth] = lo
-            p3[i * LANES : (i + 1) * LANES, 2 * depth : 3 * depth] = hi
-
-    def work(block, q_block):
-        base = pl.multiple_of(block * pb, LANES)
+    def prepare(halves):
+        for u, (block, ref, part) in enumerate(halves):
+            base = pl.multiple_of(block * pb + part * hb, LANES)
+            for i in range(hb // LANES):
+                x = ref[part * hb + i * LANES : part * hb + (i + 1) * LANES, :]
+                norm = norms(x)
+                lane = part * hb // LANES + i
+                pn[block, lane : lane + 1, :] = norm
+                g8[:, pl.ds(pl.multiple_of(base + i * LANES, LANES), LANES)] = jnp.broadcast_to(
+                    -norm * kappa1, (8, LANES)
+                )
+                hi = x.astype(jnp.bfloat16)
+                lo = (x - hi.astype(jnp.float32)).astype(jnp.bfloat16)
+                here = slice(u * hb + i * LANES, u * hb + (i + 1) * LANES)
+                p3[here, 0:depth] = hi
+                p3[here, depth : 2 * depth] = lo
+                p3[here, 2 * depth : 3 * depth] = hi
+
+    def work(halves, q_block):
         top = pl.multiple_of(q_block * qb, qb)
-        tile[pl.ds(top, qb), pl.ds(base, pb)] = lax.dot_general(
+        bases = [pl.multiple_of(block * pb + part * hb, LANES) for block, _, part in halves]
+        lanes = [
+            pl.ds(pl.multiple_of(base + k * LANES, LANES), LANES)
+            for base in bases
+            for k in range(hb // LANES)
+        ]
+        product = lax.dot_general(
             q3[pl.ds(top, qb), :], p3[...], (((1,), (1,)), ((), ())),
             preferred_element_type=jnp.float32,
         )
+        for u, base in enumerate(bases):
+            tile[pl.ds(top, qb), pl.ds(base, hb)] = product[:, u * hb : (u + 1) * hb]
 
         def first(i, _):
-            g = [g8[:, pl.ds(pl.multiple_of(base + k * LANES, LANES), LANES)] for k in range(wide)]
+            g = [g8[:, lane] for lane in lanes]
             for r in range(16):
                 at_row = pl.ds(pl.multiple_of(top + i * 128 + r * 8, 8), 8)
-                z = [
-                    tile[at_row, pl.ds(pl.multiple_of(base + k * LANES, LANES), LANES)] + g[k]
-                    for k in range(wide)
-                ]
+                z = [tile[at_row, lane] + g[k] for k, lane in enumerate(lanes)]
                 m_rows[at_row, :], s_rows[at_row, :] = online(m_rows[at_row, :], s_rows[at_row, :], z)
             return 0
 
@@ -295,12 +304,14 @@
 
         lax.fori_loop(0, h_cols // (side * LANES), strip, 0)
 
-    prepare(row, p_ref)
+    mine = [(row, p_ref, 0), (row, p_ref, 1)]
+    prepare(mine)
     split_q(col, q_ref)
-    work(row, col)
+    work(mine, col)
     own.wait_recv()
     split_q(sibling, qbuf.at[sibling])
-    work(row, sibling)
+    work(mine, sibling)
+    pass_on(1, 0)
     for d, c in enumerate(cross, 1):
         c.wait_recv()
         source = lax.rem(col - 2 * d + nc, nc)
@@ -310,50 +321,38 @@
         )
         fwd.start()
         passed.append(fwd)
-        if d == 1:
-            for r in steps[1]:
-                r.wait_recv()
-            steps[2] = ring(2)
-            for r in steps[2]:
-                r.start()
         split_q(source, qbuf.at[source])
-        work(row, source)
+        work(mine, source)
+    pass_on(1, 1)
     for d, c in enumerate(passed, 1):
         c.wait_recv()
         source = lax.rem(sibling - 2 * d + nc, nc)
         split_q(source, qbuf.at[source])
-        work(row, source)
-
-    def all_queries(owner):
-        prepare(owner, pbuf.at[owner])
-
+        work(mine, source)
+
+    def some_queries(halves, start, end):
         def body(i, _):
-            work(owner, i)
+            work(halves, i)
             return 0
 
-        lax.fori_loop(0, nc, body, 0)
+        lax.fori_loop(start, end, body, 0)
 
     for step in range(1, half):
-        if step > 1:
-            for c in steps[step]:
-                c.wait_recv()
-            steps[step + 1] = ring(step + 1)
-            for c in steps[step + 1]:
-                c.start()
-        for owner in (at(pos - step), at(pos + step)):
-            all_queries(owner)
-    for c in steps[half]:
+        for turn in range(2):
+            if step > 1:
+                pass_on(step, turn)
+            left, right = at(pos - step), at(pos + step)
+            halves = [(left, pbuf.at[left], turn), (right, pbuf.at[right], 1 - turn)]
+            prepare(halves)
+            some_queries(halves, 0, nc)
+    for c in steps[half, 0]:
         c.wait_recv()
-    owner = at(pos + half)
-    prepare(owner, pbuf.at[owner])
+    last = at(pos + half)
+    halves = [(last, pbuf.at[last], 0), (last, pbuf.at[last], 1)]
+    prepare(halves)
     row_copies = []
     for h in range(2):
-
-        def body(i, _):
-            work(owner, i)
-            return 0
-
-        lax.fori_loop(h * nc // 2, (h + 1) * nc // 2, body, 0)
+        some_queries(halves, h * nc // 2, (h + 1) * nc // 2)
         row_copies.append(send_rows(0, h))
 
     for t in range(ITERS):
@@ -382,8 +381,8 @@
         c.wait_send()
     for c in cross + [own] + passed:
         c.wait_send()
-    for step in range(1, half + 1):
-        for c in steps[step]:
+    for copies in steps.values():
+        for c in copies:
             c.wait_send()
 
 
@@ -421,7 +420,7 @@
             pltpu.VMEM((ITERS, nc, rows // LANES, LANES), f32),
             pltpu.VMEM((ITERS, nr, cols // LANES, LANES), f32),
             dma((nc,)), dma((nc,)),
-            dma((2, nr // 2 + 1)), dma((2, nr // 2 + 1)),
+            dma((2, nr // 2 + 1, 2)), dma((2, nr // 2 + 1, 2)),
             dma((ITERS, 2, nc)), dma((ITERS, 2, nc)),
             dma((ITERS, 2, nr)), dma((ITERS, 2, nr)),
         ],

time: 128 us -> 125 us (0.977)
  Pallas kernels: 125 us -> 122 us
    pallas_call x1, Pallas kernels: 125 us -> 122 us  [per_device(): pl.pallas_call(functools.partial(kernel, nr, nc, math.log2(qb * nr * nc),...]
where the time goes in v3:
time: 125 us
  Pallas kernels  122 us (98%)
  local copies, waits for them, and re-layouts  1.91 us (2%)
  between operations  1.29 us (1%)
    pallas_call x1, Pallas kernels, per_device(): pl.pallas_call(functools.partial(kernel, nr, nc, math.log2(qb * nr * nc),...  122 us

profile of v3, /device:TPU:0, one launch (start us, length us, event | category | flops | bytes accessed | tf_op | source)
XLA Modules:
  0.0 125.3 jit_solution(674046131045970554)
XLA Ops:
  1.3 122.1 %shard_map.50 = (f32[16,128]{1,0:T(8,128)}, f32[32,128]{1,0:T(8,128)}) custom-call(f32[1]{0:T(128)S(6)} %copy.7.mc_ref, f32[512,256]{1,0:T(8,128)} %q_ref.1, f32[512,256]{1,0:T(8,128)} %p_ref.1), custom_call_target="tpu_custom_call" | custom-call | flops 12884901888 | bytes 1048576 | tf_op jit(solution)/shard_map/pallas_call | solution.py:396
  123.4 0.0 copy-start
  123.4 1.3 %copy.8 = f32[2048]{0:T(1024)} copy(f32[2048]{0:T(1024)} %bitcast.3) | data formatting | bytes 16384
  124.7 0.0 copy-done
  124.7 0.6 copy.9
Async XLA Ops:
  123.4 1.3 %copy-start = (f32[32,128]{1,0:T(8,128)S(1)}, f32[32,128]{1,0:T(8,128)}, u32[]{:S(2)}) copy-start(f32[32,128]{1,0:T(8,128)} %get-tuple-element.5) | copy-start | bytes 49156

commit v4 on v3

--- a/solution.py
+++ b/solution.py
@@ -153,12 +153,14 @@
                 g8[:, pl.ds(pl.multiple_of(base + i * LANES, LANES), LANES)] = jnp.broadcast_to(
                     -norm * kappa1, (8, LANES)
                 )
-                hi = x.astype(jnp.bfloat16)
-                lo = (x - hi.astype(jnp.float32)).astype(jnp.bfloat16)
                 here = slice(u * hb + i * LANES, u * hb + (i + 1) * LANES)
-                p3[here, 0:depth] = hi
-                p3[here, depth : 2 * depth] = lo
-                p3[here, 2 * depth : 3 * depth] = hi
+                for k in range(depth // LANES):
+                    v = x[:, k * LANES : (k + 1) * LANES].T
+                    hi = v.astype(jnp.bfloat16)
+                    lo = (v - hi.astype(jnp.float32)).astype(jnp.bfloat16)
+                    for piece, value in enumerate((hi, lo, hi)):
+                        spot = piece * depth + k * LANES
+                        p3[spot : spot + LANES, here] = value
 
     def work(halves, q_block):
         top = pl.multiple_of(q_block * qb, qb)
@@ -169,7 +171,7 @@
             for k in range(hb // LANES)
         ]
         product = lax.dot_general(
-            q3[pl.ds(top, qb), :], p3[...], (((1,), (1,)), ((), ())),
+            q3[pl.ds(top, qb), :], p3[...], (((1,), (0,)), ((), ())),
             preferred_element_type=jnp.float32,
         )
         for u, base in enumerate(bases):
@@ -276,7 +278,7 @@
                 m_rows[at_row, :], s_rows[at_row, :] = pair[r]
             return 0
 
-        lax.fori_loop(0, h_rows // 32, body, 0, unroll=2)
+        lax.fori_loop(0, h_rows // 32, body, 0, unroll=4)
 
     def col_pass(h, c):
         side = 4
@@ -297,7 +299,7 @@
                 return tuple(out)
 
             start = tuple((low, zero) if h == 0 else (m_cols[:, sp], s_cols[:, sp]) for sp in lanes)
-            done = lax.fori_loop(0, h_rows // 128, body, start, unroll=2)
+            done = lax.fori_loop(0, h_rows // 128, body, start, unroll=4)
             for i in range(side):
                 m_cols[:, lanes[i]], s_cols[:, lanes[i]] = done[i]
             return 0
@@ -408,7 +410,7 @@
             pltpu.VMEM((nc, qb, depth), f32),
             pltpu.VMEM((nr, pb, depth), f32),
             pltpu.VMEM((rows, 3 * depth), bf16),
-            pltpu.VMEM((pb, 3 * depth), bf16),
+            pltpu.VMEM((3 * depth, pb), bf16),
             pltpu.VMEM((nc, qb // LANES, LANES), f32),
             pltpu.VMEM((nr, pb // LANES, LANES), f32),
             pltpu.VMEM((8, cols), f32),

time: 125 us -> 123 us (0.984)
  Pallas kernels: 122 us -> 120 us
    pallas_call x1, Pallas kernels: 122 us -> 120 us  [per_device(): pl.pallas_call(functools.partial(kernel, nr, nc, math.log2(qb * nr * nc),...]
where the time goes in v4:
time: 123 us
  Pallas kernels  120 us (98%)
  local copies, waits for them, and re-layouts  1.91 us (2%)
  between operations  1.29 us (1%)
    pallas_call x1, Pallas kernels, per_device(): pl.pallas_call(functools.partial(kernel, nr, nc, math.log2(qb * nr * nc),...  120 us

profile of v4, /device:TPU:0, one launch (start us, length us, event | category | flops | bytes accessed | tf_op | source)
XLA Modules:
  0.0 123.0 jit_solution(2993701130073622695)
XLA Ops:
  1.3 119.8 %shard_map.50 = (f32[16,128]{1,0:T(8,128)}, f32[32,128]{1,0:T(8,128)}) custom-call(f32[1]{0:T(128)S(6)} %copy.7.mc_ref, f32[512,256]{1,0:T(8,128)} %q_ref.1, f32[512,256]{1,0:T(8,128)} %p_ref.1), custom_call_target="tpu_custom_call" | custom-call | flops 12884901888 | bytes 1048576 | tf_op jit(solution)/shard_map/pallas_call | solution.py:398
  121.1 0.0 copy-start
  121.1 1.3 %copy.8 = f32[2048]{0:T(1024)} copy(f32[2048]{0:T(1024)} %bitcast.3) | data formatting | bytes 16384
  122.4 0.0 copy-done
  122.4 0.6 copy.9
Async XLA Ops:
  121.1 1.3 %copy-start = (f32[32,128]{1,0:T(8,128)S(1)}, f32[32,128]{1,0:T(8,128)}, u32[]{:S(2)}) copy-start(f32[32,128]{1,0:T(8,128)} %get-tuple-element.5) | copy-start | bytes 49156
